TPU v7x, 256 devices: a whole 4x4x8 slice. The times are simulated.
256 devices in a mesh: gx: 4 (over z_lo), gy: 8 (over y, z_hi), gz: 8 (over x, core).
Axes of the slice: x: 4, y: 4, z: 8 (z_hi: 2, z_lo: 4; z = z_hi * 4 + z_lo), core: 2. Of those that a mesh axis runs over, the one named last changes fastest.
Arguments:
- inputs: float32 [2048, 4096], P('gz', 'gx'), may hold values from -6 to 6
- pre_act: float32 [2048, 8192], P('gz', 'gy'), may hold values from -6 to 6
- w_in: float32 [4096, 8192], P('gx', 'gy'), may hold values from -0.75 to 0.75
- w_out: float32 [8192, 4096], P('gy', 'gx'), may hold values from -0.0625 to 0.0625
- grad_out: float32 [2048, 4096], P('gz', 'gx'), may hold values from -0.6 to 0.6
Outputs:
- grad_inputs: float32 [2048, 4096], P('gz', ('gx', 'gy'))
- grad_w_in: float32 [4096, 8192], P('gx', ('gy', 'gz'))
- grad_w_out: float32 [8192, 4096], P(('gy', 'gz'), 'gx')
All inputs are finite; a program needn't handle non-finite values.
Results may differ from a plain program's by a relative error of at most 0.000096.
Values sent between devices are 32-bit elements; how exact they have to be, the bound alone decides.
A program may use at most 128 MiB of HBM per device.

v0:
```python
import jax
import jax.numpy as jnp
from jax import lax
from jax.sharding import PartitionSpec as P

sqrt_two_pi = 0.7978845608028654
cubic_coef = 0.044715


def gelu_value(values):
    tangent = jnp.tanh(sqrt_two_pi * (values + cubic_coef * values * values * values))
    return 0.5 * values * (1.0 + tangent)


def gelu_slope(values):
    tangent = jnp.tanh(sqrt_two_pi * (values + cubic_coef * values * values * values))
    return 0.5 * (1.0 + tangent) + 0.5 * values * (1.0 - tangent * tangent) * sqrt_two_pi * (
        1.0 + 3.0 * cubic_coef * values * values
    )


def dot_last(left, right):
    return lax.dot_general(
        left,
        right,
        (((1,), (1,)), ((), ())),
        precision=lax.Precision.HIGHEST,
        preferred_element_type=jnp.float32,
    )


def dot_first(left, right):
    return lax.dot_general(
        left,
        right,
        (((0,), (0,)), ((), ())),
        precision=lax.Precision.HIGHEST,
        preferred_element_type=jnp.float32,
    )


def per_device(inputs, pre_act, w_in, w_out, grad_out):
    partial_value = dot_last(grad_out, w_out)
    activation = gelu_value(pre_act)
    grad_act = lax.psum(partial_value, "gx")
    grad_hidden = grad_act * gelu_slope(pre_act)
    grad_inputs = lax.psum_scatter(
        dot_last(grad_hidden, w_in), "gy", scatter_dimension=1, tiled=True
    )
    hidden_cols, act_cols = (
        lax.all_to_all(grad_hidden, "gz", split_axis=1, concat_axis=0, tiled=True),
        lax.all_to_all(activation, "gz", split_axis=1, concat_axis=0, tiled=True),
    )
    grad_w_in = dot_first(lax.all_gather(inputs, "gz", axis=0, tiled=True), hidden_cols)
    grad_w_out = dot_first(act_cols, lax.all_gather(grad_out, "gz", axis=0, tiled=True))
    return (grad_inputs, grad_w_in, grad_w_out)


def solution(mesh):
    in_specs = (P("gz", "gx"), P("gz", "gy"), P("gx", "gy"), P("gy", "gx"), P("gz", "gx"))
    out_specs = (P("gz", ("gx", "gy")), P("gx", ("gy", "gz")), P(("gy", "gz"), "gx"))
    return jax.shard_map(
        per_device, mesh=mesh, in_specs=in_specs, out_specs=out_specs, check_vma=False
    )
```

profile of v0, /device:TPU:2, one launch (start us, length us, event | category | flops | bytes accessed | tf_op | source)
XLA Modules:
  0.0 192.2 jit_solution(12260439428229729464)
XLA Ops:
  8.0 0.0 copy-start
  8.0 0.0 all-reduce.2.cloned.1.call-start
  8.1 7.3 %fusion.9 = f32[256,1024]{1,0:T(8,128)} fusion(f32[256,1024]{1,0:T(8,128)} %param.9, f32[1024,1024]{1,0:T(8,128)} %param.8), kind=kOutput, calls=%fused_computation.14 | convolution fusion | flops 3221225472 | bytes 6291456 | tf_op jit(solution)/shard_map/dot_general | solution.py:23
  15.3 0.0 all-reduce.2.cloned.1.call-update
  15.3 0.0 all-gather.3.cloned.1.call-start
  15.4 0.5 all-gather.3.cloned.1.call-update
  15.9 0.0 all-gather.5.cloned.1.call-start
  16.0 0.5 all-gather.5.cloned.1.call-update
  16.5 65.9 %all-reduce.2.cloned.1.call-done = f32[256,1024]{1,0:T(8,128)} async-done(((f32[256,1024]{1,0:T(8,128)}), f32[256,1024]{1,0:T(8,128)}) %all-reduce.2.cloned.1.call-update) | async-done | bytes 1048592 | tf_op jit(solution)/shard_map/psum | solution.py:45
  82.4 0.0 copy-done
  82.4 0.0 copy-start.1
  82.4 3.0 %multiply_bitcast_fusion = (f32[32,8,8,128]{3,2,1,0:T(8,128)}, f32[32,8,8,128]{3,2,1,0:T(8,128)S(1)}) fusion(f32[256,1024]{1,0:T(8,128)S(1)} %copy-done, f32[256,1024]{1,0:T(8,128)} %all-reduce.2.cloned.1.call-done), kind=kLoop, calls=%fused_computation.11 | loop fusion | flops 4980736 | bytes 4194304
  85.4 1.0 copy.17
  86.5 4.8 %all-to-all-start = ((f32[256,8,128]{2,0,1:T(8,128)}), f32[256,8,128]{2,0,1:T(8,128)S(1)}, u32[]{:S(2)}, u32[]{:S(2)}) async-start(f32[256,8,128]{2,0,1:T(8,128)} %bitcast.27), calls=%async_computation.1 | async-start | bytes 2097152 | tf_op jit(solution)/shard_map/all_to_all | solution.py:51
  91.3 0.0 reduce-scatter.2.cloned.1.call-start
  91.3 0.0 copy-done.1
  91.3 7.4 %fusion.7 = f32[256,1024]{1,0:T(8,128)} fusion(f32[1024,1024]{1,0:T(8,128)} %param.7, f32[256,1024]{1,0:T(8,128)S(1)} %copy-done.1, f32[256,1024]{1,0:T(8,128)S(1)} %copy-done), kind=kOutput, calls=%fused_computation.13 | convolution fusion | flops 3225944064 | bytes 7340032 | tf_op jit(solution)/shard_map/dot_general | solution.py:23
  98.7 0.0 reduce-scatter.2.cloned.1.call-update
  98.7 2.3 %copy.16 = f32[32,8,8,128]{3,2,0,1:T(8,128)} copy(f32[32,8,8,128]{3,2,1,0:T(8,128)} %get-tuple-element.9) | data formatting | bytes 2097152 | tf_op jit(solution)/shard_map/all_to_all | solution.py:52
  101.0 16.3 %all-to-all-done = f32[256,8,128]{2,0,1:T(8,128)S(1)} async-done(((f32[256,8,128]{2,0,1:T(8,128)}), f32[256,8,128]{2,0,1:T(8,128)S(1)}, u32[]{:S(2)}, u32[]{:S(2)}) %all-to-all-start) | async-done | bytes 1048608 | tf_op jit(solution)/shard_map/all_to_all | solution.py:51
  117.3 5.0 %all-to-all-start.1 = ((f32[256,8,128]{2,0,1:T(8,128)}), f32[256,8,128]{2,0,1:T(8,128)S(1)}, u32[]{:S(2)}, u32[]{:S(2)}) async-start(f32[256,8,128]{2,0,1:T(8,128)} %bitcast.23), calls=%async_computation.2 | async-start | bytes 2097152 | tf_op jit(solution)/shard_map/all_to_all | solution.py:52
  122.3 0.0 all-gather.3.cloned.1.call-done
  122.3 7.6 %convolution_bitcast_fusion = f32[1024,128]{0,1:T(8,128)S(1)} fusion(f32[2048,128]{1,0:T(8,128)S(1)} %bitcast.25, f32[2048,1024]{1,0:T(8,128)} %all-gather.3.cloned.1.call-done), kind=kOutput, calls=%fused_computation.2 | convolution fusion | flops 3221225472 | bytes 9961472 | tf_op jit(solution)/shard_map/dot_general | solution.py:33
  129.9 1.0 copy.11
  130.9 16.6 %all-to-all-done.1 = f32[256,8,128]{2,0,1:T(8,128)S(1)} async-done(((f32[256,8,128]{2,0,1:T(8,128)}), f32[256,8,128]{2,0,1:T(8,128)S(1)}, u32[]{:S(2)}, u32[]{:S(2)}) %all-to-all-start.1) | async-done | bytes 1048608 | tf_op jit(solution)/shard_map/all_to_all | solution.py:52
  147.5 0.0 all-gather.5.cloned.1.call-done
  147.5 7.8 %fusion.10 = f32[128,1024]{1,0:T(8,128)} fusion(f32[2048,128]{1,0:T(8,128)S(1)} %bitcast.26, f32[2048,1024]{1,0:T(8,128)} %all-gather.5.cloned.1.call-done), kind=kOutput, calls=%fused_computation.15 | convolution fusion | flops 3221225472 | bytes 9961472 | tf_op jit(solution)/shard_map/dot_general | solution.py:33
  155.3 29.4 %reduce-scatter.2.cloned.1.call-done = f32[256,128]{1,0:T(8,128)} async-done(((f32[256,1024]{1,0:T(8,128)}), f32[256,128]{1,0:T(8,128)}) %reduce-scatter.2.cloned.1.call-update) | async-done | bytes 131088 | tf_op jit(solution)/shard_map/reduce_scatter | solution.py:47
Async XLA Ops:
  8.0 74.4 %copy-start = (f32[256,1024]{1,0:T(8,128)S(1)}, f32[256,1024]{1,0:T(8,128)}, u32[]{:S(2)}) copy-start(f32[256,1024]{1,0:T(8,128)} %param.6) | copy-start | bytes 3145732
  8.0 74.4 %all-reduce.2.cloned.1.call-start = ((), (), s32[]{:S(2)}) async-start(), calls=%async_computation.3 | async-start | bytes 2097152 | tf_op jit(solution)/shard_map/psum | solution.py:45
  15.3 107.0 %all-gather.3.cloned.1.call-start = ((), (), s32[]{:S(2)}) async-start(), calls=%async_computation.5 | async-start | bytes 9437184 | tf_op jit(solution)/shard_map/all_gather | solution.py:54
  15.9 131.6 %all-gather.5.cloned.1.call-start = ((), (), s32[]{:S(2)}) async-start(), calls=%async_computation.6 | async-start | bytes 9437184 | tf_op jit(solution)/shard_map/all_gather | solution.py:55
  82.4 8.8 %copy-start.1 = (f32[256,1024]{1,0:T(8,128)S(1)}, f32[256,1024]{1,0:T(8,128)}, u32[]{:S(2)}) copy-start(f32[256,1024]{1,0:T(8,128)} %all-reduce.2.cloned.1.call-done) | copy-start | bytes 3145732
  86.5 30.9 %all-to-all-start = ((f32[256,8,128]{2,0,1:T(8,128)}), f32[256,8,128]{2,0,1:T(8,128)S(1)}, u32[]{:S(2)}, u32[]{:S(2)}) async-start(f32[256,8,128]{2,0,1:T(8,128)} %bitcast.27), calls=%async_computation.1 | async-start | bytes 2097152 | tf_op jit(solution)/shard_map/all_to_all | solution.py:51
  91.3 93.5 %reduce-scatter.2.cloned.1.call-start = ((), (), s32[]{:S(2)}) async-start(), calls=%async_computation.4 | async-start | bytes 1179648 | tf_op jit(solution)/shard_map/reduce_scatter | solution.py:47
  117.3 30.1 %all-to-all-start.1 = ((f32[256,8,128]{2,0,1:T(8,128)}), f32[256,8,128]{2,0,1:T(8,128)S(1)}, u32[]{:S(2)}, u32[]{:S(2)}) async-start(f32[256,8,128]{2,0,1:T(8,128)} %bitcast.23), calls=%async_computation.2 | async-start | bytes 2097152 | tf_op jit(solution)/shard_map/all_to_all | solution.py:52
Sparse Core Ops, SparseCore 0:
  15.5 66.9 all-reduce.1
  98.8 85.8 reduce-scatter.1
Sparse Core Ops, SparseCore 1:
  17.7 54.2 all-gather.2
  73.7 73.4 all-gather.4
where the time goes:
time: 192 us
  waiting for transfers between devices  129 us (67%)
  matrix products  30 us (16%)
  between operations  15.5 us (8%)
  starting transfers between devices  9.92 us (5%)
  local copies, waits for them, and re-layouts  4.34 us (2%)
  other arithmetic  2.99 us (2%)
    psum x1, waiting for transfers between devices, per_device(): grad_act = lax.psum(partial_value, 'gx')  65.9 us
    reduce_scatter x1, waiting for transfers between devices, per_device(): lax.psum_scatter(dot_last(grad_hidden, w_in), 'gy', scatter_dimension=1,...  29.4 us
    all_to_all x1, waiting for transfers between devices, per_device(): lax.all_to_all(activation, 'gz', split_axis=1, concat_axis=0, tiled=True)  16.6 us
    all_to_all x1, waiting for transfers between devices, per_device(): lax.all_to_all(grad_hidden, 'gz', split_axis=1, concat_axis=0, tiled=True)  16.3 us
    dot_general x2, matrix products, dot_first(): lax.dot_general(left, right, (((0,), (0,)), ((), ())), precision=lax.Prec...  15.4 us
    dot_general x2, matrix products, dot_last(): lax.dot_general(left, right, (((1,), (1,)), ((), ())), precision=lax.Prec...  14.7 us
    all_to_all x1, starting transfers between devices, per_device(): lax.all_to_all(activation, 'gz', split_axis=1, concat_axis=0, tiled=True)  4.99 us
    all_to_all x1, starting transfers between devices, per_device(): lax.all_to_all(grad_hidden, 'gz', split_axis=1, concat_axis=0, tiled=True)  4.81 us
  transfers between devices with their start and end apart: 6, of which 4 were waited for; matrix products, arithmetic and copies ran while one was open for 16% of the time, Pallas kernels for 0%

commit v1 on v0

v1 whole, which is shorter than its diff:
```python
import functools

import jax
import jax.numpy as jnp
from jax import lax
from jax.experimental import pallas as pl
from jax.experimental.pallas import tpu as pltpu
from jax.sharding import PartitionSpec as P

MESH = pl.DeviceIdType.MESH
F32 = jnp.float32
BF16 = jnp.bfloat16
sqrt_two_pi = 0.7978845608028654
cubic_coef = 0.044715

TOK = 256
WID = 1024
BLK = 128
HALF = 512
PARTS = 2
ROWS = TOK // PARTS
CHUNKS = [(k, e, t) for t in range(PARTS) for k in range(4) for e in range(2)]
LAG = 2
FLIGHT = 3

NN = (((1,), (0,)), ((), ()))
NT = (((1,), (1,)), ((), ()))


def split(value):
    high = value.astype(BF16)
    return high, (value - high.astype(F32)).astype(BF16)


def dot3(left, right, dims):
    (lh, ll), (rh, rl) = left, right
    d = lambda a, b: lax.dot_general(a, b, dims, preferred_element_type=F32)
    return d(lh, rh) + (d(lh, rl) + d(ll, rh))


def tangent_of(v):
    return jnp.tanh(sqrt_two_pi * (v + cubic_coef * v * v * v))


def gelu_value(v, t):
    return 0.5 * v * (1.0 + t)


def gelu_slope(v, t):
    return 0.5 * (1.0 + t) + 0.5 * v * (1.0 - t * t) * sqrt_two_pi * (1.0 + 3.0 * cubic_coef * v * v)


def kernel(
    x_in, p_in, wi_in, wo_in, g_in, gi_out, gwi_out, gwo_out,
    g_v, gs_v, g_h, g_l, wo_v, wo_h, wo_l, wi_v, wi_h, wi_l, x_v, xs_v, x_h, x_l,
    p_v, ps_v, der_v, a_h, a_l, h_h, h_l, own_z, rp, rs, sp, ss, hid_h, hid_l, hsend, hs_v,
    xsend, xrecv, xown, ysend, yrecv, yown, hsnd, hrcv, gi_v, gwi_v, gwo_v,
    lsem, osem, csend, crecv, zsend, zrecv, xss, xrs, yss, yrs, vss, vrs,
):
    gx, gy, gz = lax.axis_index("gx"), lax.axis_index("gy"), lax.axis_index("gz")
    y, zh, x, c = gy // 2, gy % 2, gz // 2, gz % 2
    xp, xm, xo = (x + 1) % 4, (x + 3) % 4, (x + 2) % 4
    yp, ym, yo = (y + 1) % 4, (y + 3) % 4, (y + 2) % 4
    owners = (xo, xp, xm, x)
    yowners = (yo, yp, ym, y)
    sibling = (gx, gy, x * 2 + 1 - c)
    x_next, x_prev = (gx, gy, xp * 2 + c), (gx, gy, xm * 2 + c)
    y_next, y_prev = (gx, yp * 2 + zh, gz), (gx, ym * 2 + zh, gz)
    partner = (gx, y * 2 + 1 - zh, gz)
    zr, zl = (gx + 1) % 4, (gx + 3) % 4
    z_next = (zr, y * 2 + jnp.where(gx == 3, 1 - zh, zh), gz)
    z_prev = (zl, y * 2 + jnp.where(gx == 0, 1 - zh, zh), gz)

    def block(k, e):
        return 2 * owners[k] + (c if e else 1 - c)

    def cols(k, e):
        return pl.ds(pl.multiple_of(block(k, e) * BLK, BLK), BLK)

    def load(src, dst, n):
        return pltpu.make_async_copy(src, dst, lsem.at[n])

    l_g = load(g_in, g_v, 0)
    l_wo = [[load(wo_in.at[cols(k, e), :], wo_v.at[2 * k + e], 1 + 2 * k + e) for e in range(2)] for k in range(4)]
    l_p = [[load(p_in.at[:, cols(k, e)], p_v.at[2 * k + e], 9 + 2 * k + e) for e in range(2)] for k in range(4)]
    l_x = load(x_in, x_v, 17)
    l_wi = [
        load(wi_in.at[pl.ds(pl.multiple_of(yowners[n] * TOK, TOK), TOK), :], wi_v.at[n], 18 + n) for n in range(4)
    ]
    l_g.start()
    for k in range(4):
        for e in range(2):
            l_wo[k][e].start()
        if k == 0:
            for j in range(4):
                for e in range(2):
                    l_p[j][e].start()
    l_x.start()
    for n in range(4):
        l_wi[n].start()

    barrier = pltpu.get_barrier_semaphore()
    for who in (sibling, x_next, x_prev, y_next, y_prev, z_next, z_prev, partner):
        pl.semaphore_signal(barrier, inc=1, device_id=who, device_id_type=MESH)
    pl.semaphore_wait(barrier, 8)

    def remote(src, dst, s_sem, r_sem, who):
        return pltpu.make_async_remote_copy(
            src_ref=src, dst_ref=dst, send_sem=s_sem, recv_sem=r_sem, device_id=who, device_id_type=MESH
        )

    c_p = [remote(p_in.at[:, cols(k, 0)], ps_v.at[k], csend.at[k], crecv.at[k], sibling) for k in range(4)]
    c_g = [
        remote(g_in.at[:, pl.ds(h * HALF, HALF)], gs_v.at[h], csend.at[4 + h], crecv.at[4 + h], sibling)
        for h in range(2)
    ]
    c_x = remote(x_in, xs_v, csend.at[6], crecv.at[6], sibling)
    c_h = [remote(hsend.at[k], hs_v.at[k], csend.at[7 + k], crecv.at[7 + k], sibling) for k in range(4)]
    c_p[0].start()
    c_g[0].start()
    c_g[1].start()
    for k in range(1, 4):
        c_p[k].start()
    c_x.start()

    @pl.when(gx == 0)
    def _():
        rp[...] = jnp.zeros_like(rp)

    @pl.when(gx == 3)
    def _():
        rs[...] = jnp.zeros_like(rs)

    def where(i):
        k, e, t = CHUNKS[i]
        return (2 * k + e, pl.ds(t * ROWS, ROWS))

    def z_copy(src, dst, way, i):
        b, rows = where(i)
        return remote(
            src.at[b, rows], dst.at[b, rows], zsend.at[way, i], zrecv.at[way, i], z_next if way == 0 else z_prev
        )

    def right(i, src=None):
        return z_copy(sp if src is None else src, rp, 0, i)

    def left(i, src=None):
        return z_copy(ss if src is None else src, rs, 1, i)

    def z_own(i):
        @pl.when(gx == 0)
        def _():
            if i >= FLIGHT:
                right(i - FLIGHT).wait_send()
            right(i, own_z).start()

        @pl.when(gx == 3)
        def _():
            if i >= FLIGHT:
                left(i - FLIGHT).wait_send()
            left(i, own_z).start()

    def forward_right(i):
        b, rows = where(i)
        right(i).wait_recv()
        sp[b, rows] = own_z[b, rows] + rp[b, rows]
        right(i).start()

    def forward_left(i):
        b, rows = where(i)
        left(i).wait_recv()
        ss[b, rows] = own_z[b, rows] + rs[b, rows]
        left(i).start()

    def z_near(i):
        pl.when(gx == 1)(lambda: forward_right(i))
        pl.when(gx == 2)(lambda: forward_left(i))

    def z_far(i):
        pl.when(gx == 1)(lambda: forward_left(i))
        pl.when(gx == 2)(lambda: forward_right(i))

    def z_final(i):
        k, e, t = CHUNKS[i]
        b, rows = where(i)

        @pl.when(gx == 0)
        def _():
            left(i).wait_recv()

        @pl.when(gx == 3)
        def _():
            right(i).wait_recv()

        hidden = (own_z[b, rows] + rp[b, rows] + rs[b, rows]) * der_v[b, rows]
        high, low = split(hidden)
        hid_h[rows, cols(k, e)] = high
        hid_l[rows, cols(k, e)] = low
        if e == 0:
            hsend[k, rows] = hidden
            if t == PARTS - 1:
                c_h[k].start()
        else:
            high, low = split(hidden.T)
            h_h[k, :, rows] = high
            h_l[k, :, rows] = low

    def z_step(i):
        n = len(CHUNKS)
        if 0 <= i < n:
            z_own(i)
        if 0 <= i - 1 < n:
            z_near(i - 1)
        if 0 <= i - 1 - LAG < n:
            z_far(i - 1 - LAG)
        if 0 <= i - 1 - 2 * LAG < n:
            z_final(i - 1 - 2 * LAG)

    def partial(k):
        for e in range(2):
            l_wo[k][e].wait()
            b = 2 * k + e
            wo_h[pl.ds(b * BLK, BLK), :], wo_l[pl.ds(b * BLK, BLK), :] = split(wo_v[b])
        rows = pl.ds(2 * k * BLK, 2 * BLK)
        value = dot3((g_h[:TOK, :], g_l[:TOK, :]), (wo_h[rows, :], wo_l[rows, :]), NT)
        own_z[2 * k] = value[:, :BLK]
        own_z[2 * k + 1] = value[:, BLK:]

    def gelu(k):
        for e in range(2):
            l_p[k][e].wait()
            v = p_v[2 * k + e]
            t = tangent_of(v)
            der_v[2 * k + e] = gelu_slope(v, t)
            if e == 1:
                a_h[k, :, :TOK], a_l[k, :, :TOK] = split(gelu_value(v, t).T)
        c_p[k].wait_recv()
        v = ps_v[k]
        a_h[k, :, TOK:], a_l[k, :, TOK:] = split(gelu_value(v, tangent_of(v)).T)

    def x_copy(g, m):
        return remote(xsend.at[g, m], xrecv.at[g, m], xss.at[g, m], xrs.at[g, m], x_next if m % 2 == 0 else x_prev)

    def weight(g, k, h):
        th, tl, vh, vl = (a_h, a_l, g_h, g_l) if g == 0 else (h_h, h_l, x_h, x_l)
        half = pl.ds(h * HALF, HALF)
        return dot3((th[k], tl[k]), (vh[:, half], vl[:, half]), NN)

    def x_send(g, m, k, h):
        xsend[g, m] = weight(g, k, h)
        x_copy(g, m).start()

    def x_first(g):
        x_send(g, 1, 0, 0)
        x_send(g, 0, 0, 1)

    def x_second(g):
        x_send(g, 2, 1, 0)
        x_send(g, 3, 2, 1)

    def x_third_local(g):
        xsend[g, 4] = weight(g, 1, 1)
        xsend[g, 5] = weight(g, 2, 0)

    def x_third(g):
        for m in (4, 5):
            x_copy(g, m - 4).wait_recv()
            xsend[g, m] = xsend[g, m] + xrecv[g, m - 4]
            x_copy(g, m).start()

    def x_own(g):
        xown[g, 0] = weight(g, 3, 0)
        xown[g, 1] = weight(g, 3, 1)

    def x_final(g):
        for h, ms in ((0, (2, 5)), (1, (3, 4))):
            for m in ms:
                x_copy(g, m).wait_recv()
            total = xown[g, h] + xrecv[g, ms[0]] + xrecv[g, ms[1]]
            half = pl.ds(h * HALF, HALF)
            if g == 0:
                gwo_v[:, half] = total
            else:
                gwi_v[half, :] = total.T
        if g == 0:
            pltpu.make_async_copy(gwo_v, gwo_out, osem.at[0]).start()
        else:
            pltpu.make_async_copy(gwi_v, gwi_out, osem.at[1]).start()

    def hidden_sibling(k):
        c_h[k].wait_recv()
        h_h[k, :, TOK:], h_l[k, :, TOK:] = split(hs_v[k].T)

    def split_inputs():
        l_x.wait()
        x_h[:TOK, :], x_l[:TOK, :] = split(x_v[...])
        c_x.wait_recv()
        x_h[TOK:, :], x_l[TOK:, :] = split(xs_v[...])

    def split_w_in(n):
        l_wi[n].wait()
        wi_h[n], wi_l[n] = split(wi_v[n])

    QR = ROWS // 2

    def y_copy(t, m):
        return remote(ysend.at[t, m], yrecv.at[t, m], yss.at[t, m], yrs.at[t, m], y_next if m % 2 == 0 else y_prev)

    def y_block(t, n):
        rows = pl.ds(t * ROWS, ROWS)
        return dot3((hid_h[rows, :], hid_l[rows, :]), (wi_h[n], wi_l[n]), NT)

    def y_send(t, m, value):
        ysend[t, m] = value
        y_copy(t, m).start()

    def y_first(t):
        v = y_block(t, 0)
        y_send(t, 1, v[:QR])
        y_send(t, 0, v[QR:])

    def y_second(t):
        v = y_block(t, 1)
        y_send(t, 2, v[:QR])
        ysend[t, 4] = v[QR:]
        v = y_block(t, 2)
        y_send(t, 3, v[QR:])
        ysend[t, 5] = v[:QR]

    def y_third(t):
        for m in (4, 5):
            y_copy(t, m - 4).wait_recv()
            ysend[t, m] = ysend[t, m] + yrecv[t, m - 4]
            y_copy(t, m).start()

    def y_own(t):
        yown[t] = y_block(t, 3)

    def v_copy(t):
        return remote(hsnd.at[t], hrcv.at[t], vss.at[t], vrs.at[t], partner)

    def y_final(t):
        for h, ms in ((0, (2, 5)), (1, (3, 4))):
            for m in ms:
                y_copy(t, m).wait_recv()
            rows = pl.ds(h * QR, QR)
            total = yown[t, rows] + yrecv[t, ms[0]] + yrecv[t, ms[1]]
            low, high = total[:, :BLK], total[:, BLK:]
            hsnd[t, rows] = jnp.where(zh == 0, high, low)
            gi_v[pl.ds(t * ROWS + h * QR, QR), :] = jnp.where(zh == 0, low, high)
        v_copy(t).start()

    def v_final(t):
        v_copy(t).wait_recv()
        rows = pl.ds(t * ROWS, ROWS)
        gi_v[rows, :] = gi_v[rows, :] + hrcv[t]

    l_g.wait()
    g_h[:TOK, :], g_l[:TOK, :] = split(g_v[...])
    partial(0)
    z_step(0)
    partial(1)
    z_step_own = z_step
    gelu(0)
    for h in range(2):
        c_g[h].wait_recv()
        half = pl.ds(h * HALF, HALF)
        g_h[TOK:, half], g_l[TOK:, half] = split(gs_v[h])
    x_first(0)
    z_step(1)
    partial(2)
    z_step(2)
    partial(3)
    gelu(1)
    gelu(2)
    x_second(0)
    z_step(3)
    x_third_local(0)
    z_step(4)
    gelu(3)
    z_step(5)
    x_third(0)
    z_step(6)
    x_own(0)
    z_step(7)
    split_w_in(0)
    z_step(8)
    split_w_in(1)
    z_step(9)
    split_w_in(2)
    z_step(10)
    split_w_in(3)
    z_step(11)
    split_inputs()
    z_step(12)
    y_first(0)
    z_step(13)
    y_second(0)
    z_step(14)
    hidden_sibling(0)
    x_first(1)
    y_third(0)
    z_step(15)
    x_final(0)
    z_step(16)
    y_own(0)
    z_step(17)
    z_step(18)
    hidden_sibling(1)
    hidden_sibling(2)
    x_second(1)
    z_step(19)
    z_step(20)
    y_first(1)
    y_second(1)
    x_third_local(1)
    x_third(1)
    y_third(1)
    y_final(0)
    hidden_sibling(3)
    x_own(1)
    y_own(1)
    v_final(0)
    y_final(1)
    x_final(1)
    v_final(1)
    out = pltpu.make_async_copy(gi_v, gi_out, osem.at[2])
    out.start()

    n = len(CHUNKS)
    for i in range(n):
        @pl.when((gx == 1) | (gx == 2) | ((gx == 0) & (i >= n - FLIGHT)))
        def _():
            right(i).wait_send()

        @pl.when((gx == 1) | (gx == 2) | ((gx == 3) & (i >= n - FLIGHT)))
        def _():
            left(i).wait_send()

    for copy in (*c_p, *c_g, c_x, *c_h):
        copy.wait_send()
    for m in range(6):
        for g in range(2):
            x_copy(g, m).wait_send()
        for t in range(PARTS):
            y_copy(t, m).wait_send()
    for t in range(PARTS):
        v_copy(t).wait_send()
    pltpu.make_async_copy(gwo_v, gwo_out, osem.at[0]).wait()
    pltpu.make_async_copy(gwi_v, gwi_out, osem.at[1]).wait()
    out.wait()


def per_device(inputs, pre_act, w_in, w_out, grad_out):
    v = pltpu.VMEM
    dma = pltpu.SemaphoreType.DMA
    scratch = [
        v((TOK, WID), F32), v((2, TOK, HALF), F32), v((2 * TOK, WID), BF16), v((2 * TOK, WID), BF16),
        v((8, BLK, WID), F32), v((WID, WID), BF16), v((WID, WID), BF16),
        v((4, TOK, WID), F32), v((4, TOK, WID), BF16), v((4, TOK, WID), BF16),
        v((TOK, WID), F32), v((TOK, WID), F32), v((2 * TOK, WID), BF16), v((2 * TOK, WID), BF16),
        v((8, TOK, BLK), F32), v((4, TOK, BLK), F32), v((8, TOK, BLK), F32),
        v((4, BLK, 2 * TOK), BF16), v((4, BLK, 2 * TOK), BF16), v((4, BLK, 2 * TOK), BF16), v((4, BLK, 2 * TOK), BF16),
        *[v((8, TOK, BLK), F32)] * 5,
        v((TOK, WID), BF16), v((TOK, WID), BF16), v((4, TOK, BLK), F32), v((4, TOK, BLK), F32),
        v((2, 6, BLK, HALF), F32), v((2, 6, BLK, HALF), F32), v((2, 2, BLK, HALF), F32),
        v((PARTS, 6, ROWS // 2, 2 * BLK), F32), v((PARTS, 6, ROWS // 2, 2 * BLK), F32), v((PARTS, ROWS, 2 * BLK), F32),
        v((PARTS, ROWS, BLK), F32), v((PARTS, ROWS, BLK), F32),
        v((TOK, BLK), F32), v((WID, BLK), F32), v((BLK, WID), F32),
        dma((22,)), dma((3,)), dma((11,)), dma((11,)), dma((2, len(CHUNKS))), dma((2, len(CHUNKS))),
        dma((2, 6)), dma((2, 6)), dma((PARTS, 6)), dma((PARTS, 6)), dma((PARTS,)), dma((PARTS,)),
    ]
    return pl.pallas_call(
        kernel,
        out_shape=(
            jax.ShapeDtypeStruct((TOK, BLK), F32),
            jax.ShapeDtypeStruct((WID, BLK), F32),
            jax.ShapeDtypeStruct((BLK, WID), F32),
        ),
        in_specs=[pl.BlockSpec(memory_space=pl.ANY)] * 5,
        out_specs=[pl.BlockSpec(memory_space=pl.ANY)] * 3,
        scratch_shapes=scratch,
        compiler_params=pltpu.CompilerParams(collective_id=0, has_side_effects=True, vmem_limit_bytes=60 << 20),
        cost_estimate=pl.CostEstimate(flops=6_442_450_944, bytes_accessed=13 << 20, transcendentals=1 << 19),
        name="mlp_backward",
    )(inputs, pre_act, w_in, w_out, grad_out)


def solution(mesh):
    in_specs = (P("gz", "gx"), P("gz", "gy"), P("gx", "gy"), P("gy", "gx"), P("gz", "gx"))
    out_specs = (P("gz", ("gx", "gy")), P("gx", ("gy", "gz")), P(("gy", "gz"), "gx"))
    return jax.shard_map(
        per_device, mesh=mesh, in_specs=in_specs, out_specs=out_specs, check_vma=False
    )
```

time: 192 us -> 74.3 us (0.39)
  waiting for transfers between devices: 129 us -> 0 us
  Pallas kernels: 0 us -> 68.1 us
  matrix products: 30 us -> 0 us
  between operations: 15.5 us -> 0.64 us
  starting transfers between devices: 9.92 us -> 0 us
  other arithmetic: 2.99 us -> 0 us
    pallas_call x0 -> x1, Pallas kernels: none -> 68.1 us  [per_device(): pl.pallas_call(kernel, out_shape=(jax.ShapeDtypeStruct((TOK, BLK), F32),...]
    psum x1 -> x0, waiting for transfers between devices: 65.9 us -> none  [per_device(): grad_act = lax.psum(partial_value, 'gx')]
    all_to_all x2 -> x0, waiting for transfers between devices: 32.9 us -> none  [the longest x1 16.6 us: per_device(): lax.all_to_all(activation, 'gz', split_axis=1, concat_axis=0, tiled=True)]
    dot_general x4 -> x0, matrix products: 30 us -> none  [the longest x2 15.4 us: dot_first(): lax.dot_general(left, right, (((0,), (0,)), ((), ())), precision=lax.Prec...]
    reduce_scatter x1 -> x0, waiting for transfers between devices: 29.4 us -> none  [per_device(): lax.psum_scatter(dot_last(grad_hidden, w_in), 'gy', scatter_dimension=1,...]
    all_to_all x2 -> x0, starting transfers between devices: 9.79 us -> none  [the longest x1 4.99 us: per_device(): lax.all_to_all(activation, 'gz', split_axis=1, concat_axis=0, tiled=True)]
    unnamed x5 -> x3, local copies, waits for them, and re-layouts: 1 us -> 5.32 us
    all_to_all x2 -> x0, local copies, waits for them, and re-layouts: 3.34 us -> none  [the longest x1 2.3 us: per_device(): lax.all_to_all(activation, 'gz', split_axis=1, concat_axis=0, tiled=True)]
  transfers between devices with their start and end apart: 6 -> 0, of which waited for: 4 -> 0; matrix products, arithmetic and copies ran while one was open for 16% -> 0% of each run, Pallas kernels for 0% -> 0%
where the time goes in v1:
time: 74.3 us; the launch traced here: 74.1 us
  Pallas kernels  68.1 us (92%)
  local copies, waits for them, and re-layouts  5.32 us (7%)
    pallas_call x1, Pallas kernels, per_device(): pl.pallas_call(kernel, out_shape=(jax.ShapeDtypeStruct((TOK, BLK), F32),...  68.1 us
    unnamed x3, local copies, waits for them, and re-layouts  5.32 us

profile of v1, /device:TPU:2, one launch (start us, length us, event | category | flops | bytes accessed | tf_op | source)
XLA Modules:
  0.0 74.1 jit_solution(16668526600040021641)
XLA Ops:
  0.6 68.1 %mlp_backward.1 = (f32[256,128]{1,0:T(8,128)}, f32[1024,128]{1,0:T(8,128)}, f32[128,1024]{1,0:T(8,128)}) custom-call(f32[256,1024]{1,0:T(8,128)} %x_in.1, f32[256,1024]{1,0:T(8,128)} %p_in.1, f32[1024,1024]{1,0:T(8,128)} %wi_in.1, f32[1024,1024]{1,0:T(8,128)} %wo_in.1, f32[256,1024]{1,0:T(8,128)} %g_in.1), custom_call_target="tpu_custom_call" | custom-call | flops 6442450944 | bytes 13631488 | tf_op jit(solution)/shard_map/mlp_backward/pallas_call | solution.py:473
  68.8 1.6 %copy.11 = f32[256,128]{1,0:T(8,128)} copy(f32[256,128]{1,0:T(8,128)} %get-tuple-element.6) | data formatting | bytes 262144
  70.3 1.9 %copy.12 = f32[1024,128]{1,0:T(8,128)} copy(f32[1024,128]{1,0:T(8,128)} %get-tuple-element.7) | data formatting | bytes 1048576
  72.2 1.9 %copy.13 = f32[128,1024]{1,0:T(8,128)} copy(f32[128,1024]{1,0:T(8,128)} %get-tuple-element.8) | data formatting | bytes 1048576

commit v2 on v1

--- a/solution.py
+++ b/solution.py
@@ -19,9 +19,11 @@
 HALF = 512
 PARTS = 2
 ROWS = TOK // PARTS
-CHUNKS = [(k, e, t) for t in range(PARTS) for k in range(4) for e in range(2)]
-LAG = 2
-FLIGHT = 3
+SUB = 64
+CHUNKS = [(k, e, r) for t in range(PARTS) for k in range(4) for e in range(2) for r in range(t * ROWS, (t + 1) * ROWS, SUB)]
+LAG = 5
+AHEAD = 4
+FLIGHT = 6
 
 NN = (((1,), (0,)), ((), ()))
 NT = (((1,), (1,)), ((), ()))
@@ -51,11 +53,11 @@
 
 
 def kernel(
-    x_in, p_in, wi_in, wo_in, g_in, gi_out, gwi_out, gwo_out,
+    x_in, p_in, wi_in, wo_in, g_in, gi_v, gwi_v, gwo_v,
     g_v, gs_v, g_h, g_l, wo_v, wo_h, wo_l, wi_v, wi_h, wi_l, x_v, xs_v, x_h, x_l,
     p_v, ps_v, der_v, a_h, a_l, h_h, h_l, own_z, rp, rs, sp, ss, hid_h, hid_l, hsend, hs_v,
-    xsend, xrecv, xown, ysend, yrecv, yown, hsnd, hrcv, gi_v, gwi_v, gwo_v,
-    lsem, osem, csend, crecv, zsend, zrecv, xss, xrs, yss, yrs, vss, vrs,
+    xsend, xrecv, xown, ysend, yrecv, yown, hsnd, hrcv,
+    lsem, csend, crecv, zsend, zrecv, xss, xrs, yss, yrs, vss, vrs,
 ):
     gx, gy, gz = lax.axis_index("gx"), lax.axis_index("gy"), lax.axis_index("gz")
     y, zh, x, c = gy // 2, gy % 2, gz // 2, gz % 2
@@ -132,8 +134,8 @@
         rs[...] = jnp.zeros_like(rs)
 
     def where(i):
-        k, e, t = CHUNKS[i]
-        return (2 * k + e, pl.ds(t * ROWS, ROWS))
+        k, e, r = CHUNKS[i]
+        return (2 * k + e, pl.ds(r, SUB))
 
     def z_copy(src, dst, way, i):
         b, rows = where(i)
@@ -181,7 +183,7 @@
         pl.when(gx == 2)(lambda: forward_right(i))
 
     def z_final(i):
-        k, e, t = CHUNKS[i]
+        k, e, r = CHUNKS[i]
         b, rows = where(i)
 
         @pl.when(gx == 0)
@@ -198,23 +200,25 @@
         hid_l[rows, cols(k, e)] = low
         if e == 0:
             hsend[k, rows] = hidden
-            if t == PARTS - 1:
+            if r + SUB == TOK:
                 c_h[k].start()
         else:
             high, low = split(hidden.T)
             h_h[k, :, rows] = high
             h_l[k, :, rows] = low
 
-    def z_step(i):
-        n = len(CHUNKS)
-        if 0 <= i < n:
-            z_own(i)
-        if 0 <= i - 1 < n:
-            z_near(i - 1)
-        if 0 <= i - 1 - LAG < n:
-            z_far(i - 1 - LAG)
-        if 0 <= i - 1 - 2 * LAG < n:
-            z_final(i - 1 - 2 * LAG)
+    n_chunks = len(CHUNKS)
+
+    def z_group(j):
+        for i in (2 * j, 2 * j + 1):
+            if AHEAD <= i + AHEAD < n_chunks:
+                z_own(i + AHEAD)
+            if i < n_chunks:
+                z_near(i)
+            if 0 <= i - LAG < n_chunks:
+                z_far(i - LAG)
+            if 0 <= i - 2 * LAG < n_chunks:
+                z_final(i - 2 * LAG)
 
     def partial(k):
         for e in range(2):
@@ -282,10 +286,6 @@
                 gwo_v[:, half] = total
             else:
                 gwi_v[half, :] = total.T
-        if g == 0:
-            pltpu.make_async_copy(gwo_v, gwo_out, osem.at[0]).start()
-        else:
-            pltpu.make_async_copy(gwi_v, gwi_out, osem.at[1]).start()
 
     def hidden_sibling(k):
         c_h[k].wait_recv()
@@ -358,76 +358,75 @@
     l_g.wait()
     g_h[:TOK, :], g_l[:TOK, :] = split(g_v[...])
     partial(0)
-    z_step(0)
-    partial(1)
-    z_step_own = z_step
+    for i in range(AHEAD):
+        z_own(i)
     gelu(0)
     for h in range(2):
         c_g[h].wait_recv()
         half = pl.ds(h * HALF, HALF)
         g_h[TOK:, half], g_l[TOK:, half] = split(gs_v[h])
     x_first(0)
-    z_step(1)
+    partial(1)
+    z_group(0)
     partial(2)
-    z_step(2)
+    z_group(1)
     partial(3)
+    z_group(2)
     gelu(1)
+    z_group(3)
     gelu(2)
+    z_group(4)
     x_second(0)
-    z_step(3)
+    z_group(5)
     x_third_local(0)
-    z_step(4)
+    z_group(6)
     gelu(3)
-    z_step(5)
+    z_group(7)
     x_third(0)
-    z_step(6)
+    z_group(8)
     x_own(0)
-    z_step(7)
+    z_group(9)
     split_w_in(0)
-    z_step(8)
+    z_group(10)
     split_w_in(1)
-    z_step(9)
+    z_group(11)
     split_w_in(2)
-    z_step(10)
+    z_group(12)
+    y_first(0)
+    z_group(13)
     split_w_in(3)
-    z_step(11)
+    z_group(14)
+    y_second(0)
+    z_group(15)
     split_inputs()
-    z_step(12)
-    y_first(0)
-    z_step(13)
-    y_second(0)
-    z_step(14)
+    z_group(16)
+    y_third(0)
     hidden_sibling(0)
     x_first(1)
-    y_third(0)
-    z_step(15)
-    x_final(0)
-    z_step(16)
+    z_group(17)
     y_own(0)
-    z_step(17)
-    z_step(18)
+    z_group(18)
+    z_group(19)
     hidden_sibling(1)
     hidden_sibling(2)
     x_second(1)
-    z_step(19)
-    z_step(20)
+    x_third_local(1)
+    z_group(20)
     y_first(1)
     y_second(1)
-    x_third_local(1)
     x_third(1)
     y_third(1)
     y_final(0)
+    y_own(1)
+    x_final(0)
     hidden_sibling(3)
     x_own(1)
-    y_own(1)
     v_final(0)
     y_final(1)
     x_final(1)
     v_final(1)
-    out = pltpu.make_async_copy(gi_v, gi_out, osem.at[2])
-    out.start()
-
-    n = len(CHUNKS)
+
+    n = n_chunks
     for i in range(n):
         @pl.when((gx == 1) | (gx == 2) | ((gx == 0) & (i >= n - FLIGHT)))
         def _():
@@ -446,9 +445,14 @@
             y_copy(t, m).wait_send()
     for t in range(PARTS):
         v_copy(t).wait_send()
-    pltpu.make_async_copy(gwo_v, gwo_out, osem.at[0]).wait()
-    pltpu.make_async_copy(gwi_v, gwi_out, osem.at[1]).wait()
-    out.wait()
+
+
+def write_out(*refs):
+    copies = [pltpu.make_async_copy(refs[n], refs[3 + n], refs[6].at[n]) for n in range(3)]
+    for copy in copies:
+        copy.start()
+    for copy in copies:
+        copy.wait()
 
 
 def per_device(inputs, pre_act, w_in, w_out, grad_out):
@@ -466,24 +470,28 @@
         v((2, 6, BLK, HALF), F32), v((2, 6, BLK, HALF), F32), v((2, 2, BLK, HALF), F32),
         v((PARTS, 6, ROWS // 2, 2 * BLK), F32), v((PARTS, 6, ROWS // 2, 2 * BLK), F32), v((PARTS, ROWS, 2 * BLK), F32),
         v((PARTS, ROWS, BLK), F32), v((PARTS, ROWS, BLK), F32),
-        v((TOK, BLK), F32), v((WID, BLK), F32), v((BLK, WID), F32),
-        dma((22,)), dma((3,)), dma((11,)), dma((11,)), dma((2, len(CHUNKS))), dma((2, len(CHUNKS))),
+        dma((22,)), dma((11,)), dma((11,)), dma((2, len(CHUNKS))), dma((2, len(CHUNKS))),
         dma((2, 6)), dma((2, 6)), dma((PARTS, 6)), dma((PARTS, 6)), dma((PARTS,)), dma((PARTS,)),
     ]
-    return pl.pallas_call(
+    results = pl.pallas_call(
         kernel,
-        out_shape=(
-            jax.ShapeDtypeStruct((TOK, BLK), F32),
-            jax.ShapeDtypeStruct((WID, BLK), F32),
-            jax.ShapeDtypeStruct((BLK, WID), F32),
-        ),
+        out_shape=(v((TOK, BLK), F32), v((WID, BLK), F32), v((BLK, WID), F32)),
         in_specs=[pl.BlockSpec(memory_space=pl.ANY)] * 5,
-        out_specs=[pl.BlockSpec(memory_space=pl.ANY)] * 3,
+        out_specs=[pl.BlockSpec(memory_space=pltpu.VMEM)] * 3,
         scratch_shapes=scratch,
         compiler_params=pltpu.CompilerParams(collective_id=0, has_side_effects=True, vmem_limit_bytes=60 << 20),
         cost_estimate=pl.CostEstimate(flops=6_442_450_944, bytes_accessed=13 << 20, transcendentals=1 << 19),
         name="mlp_backward",
     )(inputs, pre_act, w_in, w_out, grad_out)
+    return pl.pallas_call(
+        write_out,
+        out_shape=[jax.ShapeDtypeStruct(r.shape, F32) for r in results],
+        in_specs=[pl.BlockSpec(memory_space=pl.ANY)] * 3,
+        out_specs=[pl.BlockSpec(memory_space=pl.ANY)] * 3,
+        scratch_shapes=[dma((3,))],
+        compiler_params=pltpu.CompilerParams(vmem_limit_bytes=2 << 20),
+        name="write_out",
+    )(*results)
 
 
 def solution(mesh):

time: 74.3 us -> 64 us (0.86)
  local copies, waits for them, and re-layouts: 5.32 us -> 0 us
  Pallas kernels: 68.1 us -> 63.1 us
    unnamed x3 -> x0, local copies, waits for them, and re-layouts: 5.32 us -> none
    pallas_call x1 -> x2, Pallas kernels: 68.1 us -> 63.1 us  [the longest x1 62 us: per_device(): pl.pallas_call(kernel, out_shape=(v((TOK, BLK), F32), v((WID, BLK), F32),...]
where the time goes in v2:
time: 64 us; the launch traced here: 63.9 us
  Pallas kernels  63.1 us (99%)
  between operations  0.8 us (1%)
    pallas_call x1, Pallas kernels, per_device(): pl.pallas_call(kernel, out_shape=(v((TOK, BLK), F32), v((WID, BLK), F32),...  62 us

profile of v2, /device:TPU:2, one launch (start us, length us, event | category | flops | bytes accessed | tf_op | source)
XLA Modules:
  0.0 63.9 jit_solution(8271992931343983321)
XLA Ops:
  0.6 62.0 %mlp_backward.1 = (f32[256,128]{1,0:T(8,128)S(1)}, f32[1024,128]{1,0:T(8,128)S(1)}, f32[128,1024]{1,0:T(8,128)S(1)}) custom-call(f32[256,1024]{1,0:T(8,128)} %x_in.1, f32[256,1024]{1,0:T(8,128)} %p_in.1, f32[1024,1024]{1,0:T(8,128)} %wi_in.1, f32[1024,1024]{1,0:T(8,128)} %wo_in.1, f32[256,1024]{1,0:T(8,128)} %g_in.1), custom_call_target="tpu_custom_call" | custom-call | flops 6442450944 | bytes 13631488 | tf_op jit(solution)/shard_map/mlp_backward/pallas_call | solution.py:476
  62.7 1.0 %write_out.1 = (f32[256,128]{1,0:T(8,128)}, f32[1024,128]{1,0:T(8,128)}, f32[128,1024]{1,0:T(8,128)}) custom-call(f32[256,128]{1,0:T(8,128)S(1)} %get-tuple-element.6.refs_0_, f32[1024,128]{1,0:T(8,128)S(1)} %get-tuple-element.7.refs_1_, f32[128,1024]{1,0:T(8,128)S(1)} %get-tuple-element.8.refs_2_), custom_call_target="tpu_custom_call" | custom-call | tf_op jit(solution)/shard_map/write_out/pallas_call | solution.py:486

commit v3 on v2

--- a/solution.py
+++ b/solution.py
@@ -57,7 +57,7 @@
     g_v, gs_v, g_h, g_l, wo_v, wo_h, wo_l, wi_v, wi_h, wi_l, x_v, xs_v, x_h, x_l,
     p_v, ps_v, der_v, a_h, a_l, h_h, h_l, own_z, rp, rs, sp, ss, hid_h, hid_l, hsend, hs_v,
     xsend, xrecv, xown, ysend, yrecv, yown, hsnd, hrcv,
-    lsem, csend, crecv, zsend, zrecv, xss, xrs, yss, yrs, vss, vrs,
+    lsem, csend, crecv, zsend, zrecv, xss, xrs, yss, yrs, vss, vrs, core_in, z_in, v_in,
 ):
     gx, gy, gz = lax.axis_index("gx"), lax.axis_index("gy"), lax.axis_index("gz")
     y, zh, x, c = gy // 2, gy % 2, gz // 2, gz % 2
@@ -69,9 +69,7 @@
     x_next, x_prev = (gx, gy, xp * 2 + c), (gx, gy, xm * 2 + c)
     y_next, y_prev = (gx, yp * 2 + zh, gz), (gx, ym * 2 + zh, gz)
     partner = (gx, y * 2 + 1 - zh, gz)
-    zr, zl = (gx + 1) % 4, (gx + 3) % 4
-    z_next = (zr, y * 2 + jnp.where(gx == 3, 1 - zh, zh), gz)
-    z_prev = (zl, y * 2 + jnp.where(gx == 0, 1 - zh, zh), gz)
+    z_next, z_prev = ((gx + 1) % 4, gy, gz), ((gx + 3) % 4, gy, gz)
 
     def block(k, e):
         return 2 * owners[k] + (c if e else 1 - c)
@@ -102,9 +100,18 @@
         l_wi[n].start()
 
     barrier = pltpu.get_barrier_semaphore()
-    for who in (sibling, x_next, x_prev, y_next, y_prev, z_next, z_prev, partner):
-        pl.semaphore_signal(barrier, inc=1, device_id=who, device_id_type=MESH)
-    pl.semaphore_wait(barrier, 8)
+    def tell(sem, who):
+        pl.semaphore_signal(sem, inc=1, device_id=who, device_id_type=MESH)
+
+    for who in (x_next, x_prev, y_next, y_prev):
+        tell(barrier, who)
+    pl.when(c == 0)(lambda: tell(barrier, sibling))
+    pl.when(gx < 3)(lambda: tell(barrier, z_next))
+    pl.when(zh == 0)(lambda: tell(barrier, partner))
+    pl.semaphore_wait(barrier, 4 + c + jnp.where(gx > 0, 1, 0) + zh)
+    pl.when(c == 1)(lambda: tell(core_in, sibling))
+    pl.when(gx > 0)(lambda: tell(z_in, z_prev))
+    pl.when(zh == 1)(lambda: tell(v_in, partner))
 
     def remote(src, dst, s_sem, r_sem, who):
         return pltpu.make_async_remote_copy(
@@ -118,12 +125,14 @@
     ]
     c_x = remote(x_in, xs_v, csend.at[6], crecv.at[6], sibling)
     c_h = [remote(hsend.at[k], hs_v.at[k], csend.at[7 + k], crecv.at[7 + k], sibling) for k in range(4)]
-    c_p[0].start()
-    c_g[0].start()
-    c_g[1].start()
-    for k in range(1, 4):
-        c_p[k].start()
-    c_x.start()
+    def greet_sibling():
+        pl.when(c == 0)(lambda: pl.semaphore_wait(core_in, 1))
+        c_p[0].start()
+        c_g[0].start()
+        c_g[1].start()
+        for k in range(1, 4):
+            c_p[k].start()
+        c_x.start()
 
     @pl.when(gx == 0)
     def _():
@@ -149,76 +158,82 @@
     def left(i, src=None):
         return z_copy(ss if src is None else src, rs, 1, i)
 
-    def z_own(i):
+    def z_own(send, i):
+        if i < n_chunks:
+            if i >= FLIGHT:
+                send(i - FLIGHT).wait_send()
+            send(i, own_z).start()
+
+    def forward(send, total, came, i):
+        if 0 <= i < n_chunks:
+            b, rows = where(i)
+            send(i).wait_recv()
+            total[b, rows] = own_z[b, rows] + came[b, rows]
+            send(i).start()
+
+    def z_begin():
         @pl.when(gx == 0)
         def _():
-            if i >= FLIGHT:
-                right(i - FLIGHT).wait_send()
-            right(i, own_z).start()
+            pl.semaphore_wait(z_in, 1)
+            for i in range(AHEAD):
+                z_own(right, i)
 
         @pl.when(gx == 3)
         def _():
-            if i >= FLIGHT:
-                left(i - FLIGHT).wait_send()
-            left(i, own_z).start()
-
-    def forward_right(i):
-        b, rows = where(i)
-        right(i).wait_recv()
-        sp[b, rows] = own_z[b, rows] + rp[b, rows]
-        right(i).start()
-
-    def forward_left(i):
-        b, rows = where(i)
-        left(i).wait_recv()
-        ss[b, rows] = own_z[b, rows] + rs[b, rows]
-        left(i).start()
-
-    def z_near(i):
-        pl.when(gx == 1)(lambda: forward_right(i))
-        pl.when(gx == 2)(lambda: forward_left(i))
-
-    def z_far(i):
-        pl.when(gx == 1)(lambda: forward_left(i))
-        pl.when(gx == 2)(lambda: forward_right(i))
-
-    def z_final(i):
-        k, e, r = CHUNKS[i]
-        b, rows = where(i)
+            for i in range(AHEAD):
+                z_own(left, i)
+
+        @pl.when((gx == 1) | (gx == 2))
+        def _():
+            pl.semaphore_wait(z_in, 1)
+
+    n_chunks = len(CHUNKS)
+
+    def z_group(j):
+        pair = (2 * j, 2 * j + 1)
+        last = [i - 2 * LAG for i in pair if 0 <= i - 2 * LAG < n_chunks]
 
         @pl.when(gx == 0)
         def _():
-            left(i).wait_recv()
+            for i in pair:
+                z_own(right, i + AHEAD)
+            for i in last:
+                left(i).wait_recv()
+
+        @pl.when(gx == 1)
+        def _():
+            for i in pair:
+                forward(right, sp, rp, i)
+                forward(left, ss, rs, i - LAG)
+
+        @pl.when(gx == 2)
+        def _():
+            for i in pair:
+                forward(left, ss, rs, i)
+                forward(right, sp, rp, i - LAG)
 
         @pl.when(gx == 3)
         def _():
-            right(i).wait_recv()
-
-        hidden = (own_z[b, rows] + rp[b, rows] + rs[b, rows]) * der_v[b, rows]
-        high, low = split(hidden)
-        hid_h[rows, cols(k, e)] = high
-        hid_l[rows, cols(k, e)] = low
-        if e == 0:
-            hsend[k, rows] = hidden
-            if r + SUB == TOK:
-                c_h[k].start()
-        else:
-            high, low = split(hidden.T)
-            h_h[k, :, rows] = high
-            h_l[k, :, rows] = low
-
-    n_chunks = len(CHUNKS)
-
-    def z_group(j):
-        for i in (2 * j, 2 * j + 1):
-            if AHEAD <= i + AHEAD < n_chunks:
-                z_own(i + AHEAD)
-            if i < n_chunks:
-                z_near(i)
-            if 0 <= i - LAG < n_chunks:
-                z_far(i - LAG)
-            if 0 <= i - 2 * LAG < n_chunks:
-                z_final(i - 2 * LAG)
+            for i in pair:
+                z_own(left, i + AHEAD)
+            for i in last:
+                right(i).wait_recv()
+
+        if last:
+            k, e, r = CHUNKS[last[0]]
+            b, rows = 2 * k + e, pl.ds(r, 2 * SUB)
+            hidden = (own_z[b, rows] + rp[b, rows] + rs[b, rows]) * der_v[b, rows]
+            high, low = split(hidden)
+            hid_h[rows, cols(k, e)] = high
+            hid_l[rows, cols(k, e)] = low
+            if e == 0:
+                hsend[k, rows] = hidden
+                if r + 2 * SUB == TOK:
+                    c_h[k].start()
+            else:
+                high, low = split(hidden.T)
+                h_h[k, :, rows] = high
+                h_l[k, :, rows] = low
 
     def partial(k):
         for e in range(2):
@@ -238,6 +253,10 @@
             der_v[2 * k + e] = gelu_slope(v, t)
             if e == 1:
                 a_h[k, :, :TOK], a_l[k, :, :TOK] = split(gelu_value(v, t).T)
+        if k > 0:
+            gelu_sibling(k)
+
+    def gelu_sibling(k):
         c_p[k].wait_recv()
         v = ps_v[k]
         a_h[k, :, TOK:], a_l[k, :, TOK:] = split(gelu_value(v, tangent_of(v)).T)
@@ -287,6 +306,14 @@
             else:
                 gwi_v[half, :] = total.T
 
+    def x_begin():
+        gelu_sibling(0)
+        for h in range(2):
+            c_g[h].wait_recv()
+            half = pl.ds(h * HALF, HALF)
+            g_h[TOK:, half], g_l[TOK:, half] = split(gs_v[h])
+        x_first(0)
+
     def hidden_sibling(k):
         c_h[k].wait_recv()
         h_h[k, :, TOK:], h_l[k, :, TOK:] = split(hs_v[k].T)
@@ -348,6 +375,8 @@
             low, high = total[:, :BLK], total[:, BLK:]
             hsnd[t, rows] = jnp.where(zh == 0, high, low)
             gi_v[pl.ds(t * ROWS + h * QR, QR), :] = jnp.where(zh == 0, low, high)
+        if t == 0:
+            pl.when(zh == 0)(lambda: pl.semaphore_wait(v_in, 1))
         v_copy(t).start()
 
     def v_final(t):
@@ -358,17 +387,14 @@
     l_g.wait()
     g_h[:TOK, :], g_l[:TOK, :] = split(g_v[...])
     partial(0)
-    for i in range(AHEAD):
-        z_own(i)
+    z_begin()
+    greet_sibling()
     gelu(0)
-    for h in range(2):
-        c_g[h].wait_recv()
-        half = pl.ds(h * HALF, HALF)
-        g_h[TOK:, half], g_l[TOK:, half] = split(gs_v[h])
-    x_first(0)
+    pl.when(c == 1)(lambda: x_begin())
     partial(1)
     z_group(0)
     partial(2)
+    pl.when(c == 0)(lambda: x_begin())
     z_group(1)
     partial(3)
     z_group(2)
@@ -426,16 +452,14 @@
     x_final(1)
     v_final(1)
 
-    n = n_chunks
-    for i in range(n):
-        @pl.when((gx == 1) | (gx == 2) | ((gx == 0) & (i >= n - FLIGHT)))
-        def _():
-            right(i).wait_send()
-
-        @pl.when((gx == 1) | (gx == 2) | ((gx == 3) & (i >= n - FLIGHT)))
-        def _():
-            left(i).wait_send()
-
+    def all_left(sends, first=0):
+        for i in range(first, n_chunks):
+            for send in sends:
+                send(i).wait_send()
+
+    pl.when(gx == 0)(lambda: all_left((right,), n_chunks - FLIGHT))
+    pl.when((gx == 1) | (gx == 2))(lambda: all_left((right, left)))
+    pl.when(gx == 3)(lambda: all_left((left,), n_chunks - FLIGHT))
     for copy in (*c_p, *c_g, c_x, *c_h):
         copy.wait_send()
     for m in range(6):
@@ -472,6 +496,7 @@
         v((PARTS, ROWS, BLK), F32), v((PARTS, ROWS, BLK), F32),
         dma((22,)), dma((11,)), dma((11,)), dma((2, len(CHUNKS))), dma((2, len(CHUNKS))),
         dma((2, 6)), dma((2, 6)), dma((PARTS, 6)), dma((PARTS, 6)), dma((PARTS,)), dma((PARTS,)),
+        *[pltpu.SemaphoreType.REGULAR] * 3,
     ]
     results = pl.pallas_call(
         kernel,

time: 64 us -> 61.1 us (0.955)
  Pallas kernels: 63.1 us -> 60.2 us
    pallas_call x1, Pallas kernels: 62 us -> 59.2 us  [per_device(): pl.pallas_call(kernel, out_shape=(v((TOK, BLK), F32), v((WID, BLK), F32),...]
where the time goes in v3:
time: 61.1 us; the launch traced here: 61 us
  Pallas kernels  60.2 us (99%)
  between operations  0.8 us (1%)
    pallas_call x1, Pallas kernels, per_device(): pl.pallas_call(kernel, out_shape=(v((TOK, BLK), F32), v((WID, BLK), F32),...  59.2 us

profile of v3, /device:TPU:2, one launch (start us, length us, event | category | flops | bytes accessed | tf_op | source)
XLA Modules:
  0.0 61.0 jit_solution(7029034722467019182)
XLA Ops:
  0.6 59.2 %mlp_backward.1 = (f32[256,128]{1,0:T(8,128)S(1)}, f32[1024,128]{1,0:T(8,128)S(1)}, f32[128,1024]{1,0:T(8,128)S(1)}) custom-call(f32[256,1024]{1,0:T(8,128)} %x_in.1, f32[256,1024]{1,0:T(8,128)} %p_in.1, f32[1024,1024]{1,0:T(8,128)} %wi_in.1, f32[1024,1024]{1,0:T(8,128)} %wo_in.1, f32[256,1024]{1,0:T(8,128)} %g_in.1), custom_call_target="tpu_custom_call" | custom-call | flops 6442450944 | bytes 13631488 | tf_op jit(solution)/shard_map/mlp_backward/pallas_call | solution.py:501
  59.8 1.0 %write_out.1 = (f32[256,128]{1,0:T(8,128)}, f32[1024,128]{1,0:T(8,128)}, f32[128,1024]{1,0:T(8,128)}) custom-call(f32[256,128]{1,0:T(8,128)S(1)} %get-tuple-element.6.refs_0_, f32[1024,128]{1,0:T(8,128)S(1)} %get-tuple-element.7.refs_1_, f32[128,1024]{1,0:T(8,128)S(1)} %get-tuple-element.8.refs_2_), custom_call_target="tpu_custom_call" | custom-call | tf_op jit(solution)/shard_map/write_out/pallas_call | solution.py:511

commit v4 on v3

--- a/solution.py
+++ b/solution.py
@@ -88,16 +88,10 @@
         load(wi_in.at[pl.ds(pl.multiple_of(yowners[n] * TOK, TOK), TOK), :], wi_v.at[n], 18 + n) for n in range(4)
     ]
     l_g.start()
-    for k in range(4):
-        for e in range(2):
-            l_wo[k][e].start()
-        if k == 0:
-            for j in range(4):
-                for e in range(2):
-                    l_p[j][e].start()
-    l_x.start()
-    for n in range(4):
-        l_wi[n].start()
+    for e in range(2):
+        l_wo[0][e].start()
+    for e in range(2):
+        l_p[0][e].start()
 
     barrier = pltpu.get_barrier_semaphore()
     def tell(sem, who):
@@ -126,13 +120,11 @@
     c_x = remote(x_in, xs_v, csend.at[6], crecv.at[6], sibling)
     c_h = [remote(hsend.at[k], hs_v.at[k], csend.at[7 + k], crecv.at[7 + k], sibling) for k in range(4)]
     def greet_sibling():
-        pl.when(c == 0)(lambda: pl.semaphore_wait(core_in, 1))
         c_p[0].start()
         c_g[0].start()
         c_g[1].start()
         for k in range(1, 4):
             c_p[k].start()
-        c_x.start()
 
     @pl.when(gx == 0)
     def _():
@@ -384,24 +376,40 @@
         rows = pl.ds(t * ROWS, ROWS)
         gi_v[rows, :] = gi_v[rows, :] + hrcv[t]
 
+    pl.when(c == 1)(greet_sibling)
     l_g.wait()
+    for k in range(1, 4):
+        for e in range(2):
+            l_wo[k][e].start()
     g_h[:TOK, :], g_l[:TOK, :] = split(g_v[...])
     partial(0)
+    for k in range(1, 4):
+        for e in range(2):
+            l_p[k][e].start()
+    l_x.start()
+    for n in range(4):
+        l_wi[n].start()
     z_begin()
-    greet_sibling()
+
+    @pl.when(c == 0)
+    def _():
+        pl.semaphore_wait(core_in, 1)
+        greet_sibling()
+
     gelu(0)
-    pl.when(c == 1)(lambda: x_begin())
+    pl.when(c == 1)(x_begin)
     partial(1)
     z_group(0)
+    pl.when(c == 0)(x_begin)
+    z_group(1)
     partial(2)
-    pl.when(c == 0)(lambda: x_begin())
-    z_group(1)
-    partial(3)
     z_group(2)
+    c_x.start()
     gelu(1)
     z_group(3)
+    partial(3)
+    z_group(4)
     gelu(2)
-    z_group(4)
     x_second(0)
     z_group(5)
     x_third_local(0)
@@ -410,40 +418,40 @@
     z_group(7)
     x_third(0)
     z_group(8)
-    x_own(0)
+    split_w_in(0)
     z_group(9)
-    split_w_in(0)
+    split_w_in(1)
     z_group(10)
-    split_w_in(1)
+    split_w_in(2)
     z_group(11)
-    split_w_in(2)
+    split_w_in(3)
     z_group(12)
     y_first(0)
     z_group(13)
-    split_w_in(3)
+    split_inputs()
     z_group(14)
     y_second(0)
     z_group(15)
-    split_inputs()
+    hidden_sibling(0)
+    x_first(1)
     z_group(16)
     y_third(0)
-    hidden_sibling(0)
-    x_first(1)
     z_group(17)
-    y_own(0)
     z_group(18)
-    z_group(19)
     hidden_sibling(1)
     hidden_sibling(2)
+    z_group(19)
     x_second(1)
-    x_third_local(1)
     z_group(20)
     y_first(1)
     y_second(1)
+    x_third_local(1)
+    y_own(0)
+    y_final(0)
     x_third(1)
     y_third(1)
-    y_final(0)
     y_own(1)
+    x_own(0)
     x_final(0)
     hidden_sibling(3)
     x_own(1)

time: 61.1 us -> 60.3 us (0.987)
  Pallas kernels: 60.2 us -> 59 us
    pallas_call x1, Pallas kernels: 59.2 us -> 57.9 us  [per_device(): pl.pallas_call(kernel, out_shape=(v((TOK, BLK), F32), v((WID, BLK), F32),...]
where the time goes in v4:
time: 60.3 us; the launch traced here: 59.8 us
  Pallas kernels  59 us (98%)
  between operations  0.8 us (1%)
    pallas_call x1, Pallas kernels, per_device(): pl.pallas_call(kernel, out_shape=(v((TOK, BLK), F32), v((WID, BLK), F32),...  57.9 us

profile of v4, /device:TPU:2, one launch (start us, length us, event | category | flops | bytes accessed | tf_op | source)
XLA Modules:
  0.0 59.8 jit_solution(1110445212476799838)
XLA Ops:
  0.6 57.9 %mlp_backward.1 = (f32[256,128]{1,0:T(8,128)S(1)}, f32[1024,128]{1,0:T(8,128)S(1)}, f32[128,1024]{1,0:T(8,128)S(1)}) custom-call(f32[256,1024]{1,0:T(8,128)} %x_in.1, f32[256,1024]{1,0:T(8,128)} %p_in.1, f32[1024,1024]{1,0:T(8,128)} %wi_in.1, f32[1024,1024]{1,0:T(8,128)} %wo_in.1, f32[256,1024]{1,0:T(8,128)} %g_in.1), custom_call_target="tpu_custom_call" | custom-call | flops 6442450944 | bytes 13631488 | tf_op jit(solution)/shard_map/mlp_backward/pallas_call | solution.py:509
  58.6 1.0 %write_out.1 = (f32[256,128]{1,0:T(8,128)}, f32[1024,128]{1,0:T(8,128)}, f32[128,1024]{1,0:T(8,128)}) custom-call(f32[256,128]{1,0:T(8,128)S(1)} %get-tuple-element.6.refs_0_, f32[1024,128]{1,0:T(8,128)S(1)} %get-tuple-element.7.refs_1_, f32[128,1024]{1,0:T(8,128)S(1)} %get-tuple-element.8.refs_2_), custom_call_target="tpu_custom_call" | custom-call | tf_op jit(solution)/shard_map/write_out/pallas_call | solution.py:519

commit v5 on v4

--- a/solution.py
+++ b/solution.py
@@ -163,21 +163,24 @@
             total[b, rows] = own_z[b, rows] + came[b, rows]
             send(i).start()
 
-    def z_begin():
+    def z_begin(first, last):
         @pl.when(gx == 0)
         def _():
-            pl.semaphore_wait(z_in, 1)
-            for i in range(AHEAD):
+            if first == 0:
+                pl.semaphore_wait(z_in, 1)
+            for i in range(first, last):
                 z_own(right, i)
 
         @pl.when(gx == 3)
         def _():
-            for i in range(AHEAD):
+            for i in range(first, last):
                 z_own(left, i)
 
-        @pl.when((gx == 1) | (gx == 2))
-        def _():
-            pl.semaphore_wait(z_in, 1)
+        if first == 0:
+
+            @pl.when((gx == 1) | (gx == 2))
+            def _():
+                pl.semaphore_wait(z_in, 1)
 
     n_chunks = len(CHUNKS)
 
@@ -237,6 +240,12 @@
         own_z[2 * k] = value[:, :BLK]
         own_z[2 * k + 1] = value[:, BLK:]
 
+    def partial_block(k, e):
+        l_wo[k][e].wait()
+        b = 2 * k + e
+        value = dot3((g_h[:TOK, :], g_l[:TOK, :]), split(wo_v[b]), NT)
+        own_z[b] = value
+
     def gelu(k):
         for e in range(2):
             l_p[k][e].wait()
@@ -382,14 +391,16 @@
         for e in range(2):
             l_wo[k][e].start()
     g_h[:TOK, :], g_l[:TOK, :] = split(g_v[...])
-    partial(0)
+    partial_block(0, 0)
+    z_begin(0, AHEAD // 2)
+    partial_block(0, 1)
     for k in range(1, 4):
         for e in range(2):
             l_p[k][e].start()
     l_x.start()
     for n in range(4):
         l_wi[n].start()
-    z_begin()
+    z_begin(AHEAD // 2, AHEAD)
 
     @pl.when(c == 0)
     def _():

time: 60.3 us -> 61.8 us (1.025)
  Pallas kernels: 59 us -> 60.1 us
    pallas_call x1, Pallas kernels: 57.9 us -> 59 us  [per_device(): pl.pallas_call(kernel, out_shape=(v((TOK, BLK), F32), v((WID, BLK), F32),...]
where the time goes in v5:
time: 61.8 us; the launch traced here: 60.9 us
  Pallas kernels  60.1 us (97%)
  between operations  0.8 us (1%)
    pallas_call x1, Pallas kernels, per_device(): pl.pallas_call(kernel, out_shape=(v((TOK, BLK), F32), v((WID, BLK), F32),...  59 us

profile of v5, /device:TPU:2, one launch (start us, length us, event | category | flops | bytes accessed | tf_op | source)
XLA Modules:
  0.0 60.9 jit_solution(11026282509187752821)
XLA Ops:
  0.6 59.0 %mlp_backward.1 = (f32[256,128]{1,0:T(8,128)S(1)}, f32[1024,128]{1,0:T(8,128)S(1)}, f32[128,1024]{1,0:T(8,128)S(1)}) custom-call(f32[256,1024]{1,0:T(8,128)} %x_in.1, f32[256,1024]{1,0:T(8,128)} %p_in.1, f32[1024,1024]{1,0:T(8,128)} %wi_in.1, f32[1024,1024]{1,0:T(8,128)} %wo_in.1, f32[256,1024]{1,0:T(8,128)} %g_in.1), custom_call_target="tpu_custom_call" | custom-call | flops 6442450944 | bytes 13631488 | tf_op jit(solution)/shard_map/mlp_backward/pallas_call | solution.py:520
  59.7 1.0 %write_out.1 = (f32[256,128]{1,0:T(8,128)}, f32[1024,128]{1,0:T(8,128)}, f32[128,1024]{1,0:T(8,128)}) custom-call(f32[256,128]{1,0:T(8,128)S(1)} %get-tuple-element.6.refs_0_, f32[1024,128]{1,0:T(8,128)S(1)} %get-tuple-element.7.refs_1_, f32[128,1024]{1,0:T(8,128)S(1)} %get-tuple-element.8.refs_2_), custom_call_target="tpu_custom_call" | custom-call | tf_op jit(solution)/shard_map/write_out/pallas_call | solution.py:530
